TPU v7x, 128 devices: a whole 4x4x4 slice. The times are simulated.
128 devices in a mesh: group: 8 (over x, core), member: 16 (over y, z).
Axes of the slice: x: 4, y: 4, z: 4, core: 2. Of those that a mesh axis runs over, the one named last changes fastest.
Arguments:
- pressure_init: float32 [262144], P(('group', 'member')), may hold values from 0.2 to 2
- gap_height: float32 [262144], P(('group', 'member'))
- active: int32 [262144], P(('group', 'member')), may hold values 0 or 1
- self_compliance: float32 [262144], P(('group', 'member')), may hold values from 1 to 3
- near_blocks: bfloat16 [1024, 9, 256, 256], P(('group', 'member')), may hold values from -0.059814453 to 0.059814453
- near_list: int32 [1024, 9], P(('group', 'member')), may hold values from 0 to 1023, as said below
- far_list: int32 [1024, 27], P(('group', 'member')), may hold values from 0 to 1023, as said below
- source_basis: bfloat16 [1024, 32, 256], P(('group', 'member')), may hold values from -0.375 to 0.375
- target_basis: bfloat16 [1024, 32, 256], P(('group', 'member')), may hold values from -0.3984375 to 0.3984375
- coupling: bfloat16 [1024, 27, 1024], P(('group', 'member')), may hold values from -0.21875 to 0.21875
Outputs:
- pressure: float32 [262144], P(('group', 'member'))
- gap: float32 [262144], P(('group', 'member'))
Inputs may be any that keep to these rules, and one draw needn't show every extreme that they name: `near_list`: slot 0 of each row is the cluster itself; the other slots name distinct clusters whose index // 128 differs from the row's own by at most one. `far_list`: each row names distinct clusters, none of them in the same row of near_list.
All inputs are finite; a program needn't handle non-finite values. No bound on the sum of `active` on one device may be relied on, other than what follows from the above.
Results may differ from a plain program's by a relative error of at most 0.0035.
Values may be sent and summed in bfloat16 or wider, within the bound.
A program may use at most 64 MiB of HBM per device.

v0:
```python
import jax
import jax.numpy as jnp
from jax import lax
from jax.sharding import PartitionSpec as P

ITERS = 2


def padded(value, sides, width):
    for axis, dim in sides:
        size, length = (lax.axis_size(axis), value.shape[dim])
        up = [(i, (i + 1) % size) for i in range(size - 1)]
        down = [(j, i) for i, j in up]
        last = lax.slice_in_dim(value, length - width, length, axis=dim)
        leading = lax.slice_in_dim(value, 0, width, axis=dim)
        before = lax.ppermute(last, axis, up)
        after = lax.ppermute(leading, axis, down)
        value = jnp.concatenate([before, value, after], axis=dim)
    return value


def shards(
    pressure_init,
    gap_height,
    active,
    self_compliance,
    near_blocks,
    near_list,
    far_list,
    source_basis,
    target_basis,
    coupling,
):
    weight = active.astype(jnp.float32)
    clusters = near_blocks.shape[0]
    cluster_size = near_blocks.shape[2]
    rank_size = source_basis.shape[1]
    far_count = far_list.shape[1]
    members = lax.axis_size("member")
    group_clusters = clusters * members
    group_index = lax.axis_index("group")
    slots = near_list - (group_index - 1) * group_clusters

    def window_of(local_rows):
        whole = lax.all_gather(local_rows, "member", axis=0, tiled=True)
        return padded(whole, (("group", 0),), group_clusters)

    def operate(direction):
        narrow = direction.astype(jnp.bfloat16)
        local_rows = narrow.reshape(clusters, cluster_size)
        projected = jnp.einsum(
            "cai,ci->ca", source_basis, local_rows, preferred_element_type=jnp.float32
        )
        outgoing = projected.astype(jnp.bfloat16).reshape(clusters * rank_size)
        all_projected = lax.all_gather(outgoing, ("group", "member"), axis=0, tiled=True).reshape(
            -1, rank_size
        )
        window = window_of(local_rows)
        near_rows = window[slots]
        near_part = jnp.einsum(
            "cnij,cnj->ci", near_blocks, near_rows, preferred_element_type=jnp.float32
        )
        picked = all_projected[far_list]
        coupled = jnp.einsum(
            "cfab,cfb->ca",
            coupling.reshape(clusters, far_count, rank_size, rank_size),
            picked,
            preferred_element_type=jnp.float32,
        ).astype(jnp.bfloat16)
        far_part = jnp.einsum(
            "cai,ca->ci", target_basis, coupled, preferred_element_type=jnp.float32
        )
        return self_compliance * narrow.astype(jnp.float32) + (near_part + far_part).reshape(-1)

    active_total = lax.psum(jnp.sum(weight), ("group", "member"))
    pressure = pressure_init * weight
    gap = operate(pressure) - gap_height
    direction = jnp.zeros_like(gap)
    norm_old = jnp.float32(1.0)
    for iteration in range(ITERS):
        gap_mean = lax.psum(jnp.sum(weight * gap), ("group", "member")) / active_total
        shifted = (gap - gap_mean) * weight
        norm_now = lax.psum(jnp.sum(shifted * shifted), ("group", "member"))
        if iteration == 0:
            direction = shifted
        else:
            direction = shifted + norm_now / norm_old * direction
        image = operate(direction)
        image_total, descent = lax.psum(
            (jnp.sum(weight * image), jnp.sum(shifted * direction)), ("group", "member")
        )
        image_mean = image_total / active_total
        curvature = lax.psum(
            jnp.sum((image - image_mean) * weight * direction), ("group", "member")
        )
        step_length = descent / curvature
        pressure = pressure - step_length * direction
        gap = gap - step_length * image
        norm_old = norm_now
    return (pressure, gap)


def solution(mesh):
    return jax.shard_map(
        shards,
        mesh=mesh,
        in_specs=(
            P(("group", "member")),
            P(("group", "member")),
            P(("group", "member")),
            P(("group", "member")),
            P(("group", "member"), None, None, None),
            P(("group", "member"), None),
            P(("group", "member"), None),
            P(("group", "member"), None, None),
            P(("group", "member"), None, None),
            P(("group", "member"), None, None),
        ),
        out_specs=(P(("group", "member")), P(("group", "member"))),
        check_vma=False,
    )
```

profile of v0, /device:TPU:1, one launch (start us, length us, event | category | flops | bytes accessed | tf_op | source)
XLA Modules:
  0.0 722.8 jit_solution(17569670003109332645)
XLA Ops:
  0.6 0.0 copy-start
  0.7 0.8 fusion.15
  1.4 20.5 %all_gather.18 = bf16[128,256]{1,0:T(8,128)(2,1)S(1)} all-gather(bf16[8,256]{1,0:T(8,128)(2,1)S(1)} %reshape.45), channel_id=1, replica_groups=mesh['group'=8,'member'=16] {'member'}, dimensions={0}, use_global_device_ids=true | all-gather | bytes 69632 | tf_op jit(solution)/shard_map/all_gather | solution.py:45
  21.9 8.1 %collective-permute-start.1 = (bf16[128,256]{1,0:T(8,128)(2,1)S(1)}, bf16[128,256]{1,0:T(8,128)(2,1)S(1)}, u32[]{:S(2)}, u32[]{:S(2)}) collective-permute-start(bf16[128,256]{1,0:T(8,128)(2,1)S(1)} %all_gather.18), channel_id=1, source_target_pairs={{16,0},{32,16},{48,32},{64,48},{80,64},{96,80},{112,96},{17,1},{33... | collective-permute-start | bytes 196616 | tf_op jit(solution)/shard_map/ppermute | solution.py:17
  30.0 3.0 collective-permute-start
  33.0 1.0 fusion.19
  34.1 0.1 reshape.118
  34.2 47.6 %all-gather = bf16[128,1,256]{2,1,0:T(2,128)(2,1)S(1)} all-gather(bf16[1,1,256]{2,1,0:T(2,128)(2,1)S(1)} %reshape.118), channel_id=1, replica_groups=mesh['group'=8,'member'=16] {'group','member'}, dimensions={0}, use_global_device_ids=true | all-gather | bytes 66048 | tf_op jit(solution)/shard_map/all_gather | solution.py:55
  81.8 0.4 reduce
  82.2 0.2 reshape.47
  82.3 0.7 compare_select_fusion
  83.0 0.1 reshape.68
  83.1 0.8 gather_fusion.1
  84.0 0.0 copy-start.6
  84.0 1.4 reshape.48
  85.4 0.6 fusion.4
  86.0 0.1 reshape.60
  86.0 0.1 fusion.13
  86.2 0.7 gather_fusion
  87.0 0.0 copy-start.1
  87.0 0.0 copy-start.3
  87.0 0.0 copy-start.7
  87.0 6.2 fusion.18
  93.3 0.6 convert_reduce_fusion
  93.9 64.7 %all-reduce.2 = (f32[]{:T(128)}, f32[]{:T(128)}) all-reduce(f32[]{:T(128)} %get-tuple-element.7, f32[]{:T(128)} %get-tuple-element.6), channel_id=1, replica_groups=mesh['group'=8,'member'=16] {'group','member'}, use_global_device_ids=true, to_apply=%region_1.0 | all-reduce | flops 2 | bytes 16 | tf_op jit(solution)/shard_map/psum | solution.py:81
  160.0 16.7 %all_gather.20 = bf16[128,256]{1,0:T(8,128)(2,1)S(1)} all-gather(bf16[8,256]{1,0:T(8,128)(2,1)S(1)} %reshape.50), channel_id=1, replica_groups=mesh['group'=8,'member'=16] {'member'}, dimensions={0}, use_global_device_ids=true | all-gather | bytes 69632 | tf_op jit(solution)/shard_map/all_gather | solution.py:45
  176.7 8.1 %collective-permute-start.3 = (bf16[128,256]{1,0:T(8,128)(2,1)S(1)}, bf16[128,256]{1,0:T(8,128)(2,1)S(1)}, u32[]{:S(2)}, u32[]{:S(2)}) collective-permute-start(bf16[128,256]{1,0:T(8,128)(2,1)S(1)} %all_gather.20), channel_id=1, source_target_pairs={{16,0},{32,16},{48,32},{64,48},{80,64},{96,80},{112,96},{17,1},{33... | collective-permute-start | bytes 196616 | tf_op jit(solution)/shard_map/ppermute | solution.py:17
  184.8 1.9 collective-permute-start.2
  186.7 0.1 fusion.21
  186.9 0.1 reshape.120
  187.0 47.9 %all-gather.1 = bf16[128,1,256]{2,1,0:T(2,128)(2,1)S(1)} all-gather(bf16[1,1,256]{2,1,0:T(2,128)(2,1)S(1)} %reshape.120), channel_id=1, replica_groups=mesh['group'=8,'member'=16] {'group','member'}, dimensions={0}, use_global_device_ids=true | all-gather | bytes 66048 | tf_op jit(solution)/shard_map/all_gather | solution.py:55
  234.9 0.4 reduce.1
  235.2 0.2 reshape.52
  235.4 0.8 gather_fusion.3
  236.3 0.6 fusion.2
  236.8 0.1 fusion.11
  237.0 0.7 gather_fusion.2
  237.8 6.2 fusion.20
  244.0 0.6 multiply_reduce_fusion.6
  244.6 64.7 %psum.76 = f32[]{:T(128)} all-reduce(f32[]{:T(128)} %get-tuple-element.20), channel_id=1, replica_groups=mesh['group'=8,'member'=16] {'group','member'}, use_global_device_ids=true, to_apply=%region_7.0 | all-reduce | flops 1 | bytes 8 | tf_op jit(solution)/shard_map/psum | solution.py:89
  310.6 0.7 multiply_reduce_fusion.5
  311.3 63.1 %all-reduce.1 = (f32[]{:T(128)}, f32[]{:T(128)}) all-reduce(f32[]{:T(128)} %get-tuple-element.5, f32[]{:T(128)} %get-tuple-element.4), channel_id=1, replica_groups=mesh['group'=8,'member'=16] {'group','member'}, use_global_device_ids=true, to_apply=%region_5.0 | all-reduce | flops 2 | bytes 16 | tf_op jit(solution)/shard_map/psum | solution.py:89
  375.7 0.6 multiply_reduce_fusion.4
  376.3 63.3 %psum.78 = f32[]{:T(128)} all-reduce(f32[]{:T(128)} %get-tuple-element.18), channel_id=1, replica_groups=mesh['group'=8,'member'=16] {'group','member'}, use_global_device_ids=true, to_apply=%region_11.0 | all-reduce | flops 1 | bytes 8 | tf_op jit(solution)/shard_map/psum | solution.py:81
  441.0 0.6 multiply_reduce_fusion.3
  441.6 63.0 %psum.79 = f32[]{:T(128)} all-reduce(f32[]{:T(128)} %get-tuple-element.16), channel_id=1, replica_groups=mesh['group'=8,'member'=16] {'group','member'}, use_global_device_ids=true, to_apply=%region_13.0 | all-reduce | flops 1 | bytes 8 | tf_op jit(solution)/shard_map/psum | solution.py:83
  505.9 17.3 %all_gather.22 = bf16[128,256]{1,0:T(8,128)(2,1)S(1)} all-gather(bf16[8,256]{1,0:T(8,128)(2,1)S(1)} %reshape.54), channel_id=1, replica_groups=mesh['group'=8,'member'=16] {'member'}, dimensions={0}, use_global_device_ids=true | all-gather | bytes 69632 | tf_op jit(solution)/shard_map/all_gather | solution.py:45
  523.2 7.9 %collective-permute-start.5 = (bf16[128,256]{1,0:T(8,128)(2,1)S(1)}, bf16[128,256]{1,0:T(8,128)(2,1)S(1)}, u32[]{:S(2)}, u32[]{:S(2)}) collective-permute-start(bf16[128,256]{1,0:T(8,128)(2,1)S(1)} %all_gather.22), channel_id=1, source_target_pairs={{16,0},{32,16},{48,32},{64,48},{80,64},{96,80},{112,96},{17,1},{33... | collective-permute-start | bytes 196616 | tf_op jit(solution)/shard_map/ppermute | solution.py:17
  531.1 1.9 collective-permute-start.4
  533.0 0.1 fusion.23
  533.2 0.1 reshape.122
  533.3 47.9 %all-gather.2 = bf16[128,1,256]{2,1,0:T(2,128)(2,1)S(1)} all-gather(bf16[1,1,256]{2,1,0:T(2,128)(2,1)S(1)} %reshape.122), channel_id=1, replica_groups=mesh['group'=8,'member'=16] {'group','member'}, dimensions={0}, use_global_device_ids=true | all-gather | bytes 66048 | tf_op jit(solution)/shard_map/all_gather | solution.py:55
  581.2 0.4 reduce.2
  581.6 0.2 reshape.56
  581.7 0.8 gather_fusion.5
  582.6 0.6 fusion
  583.1 0.2 fusion.9
  583.3 0.7 gather_fusion.4
  584.1 6.2 fusion.22
  590.3 0.6 multiply_reduce_fusion.1
  590.9 64.4 %psum.81 = f32[]{:T(128)} all-reduce(f32[]{:T(128)} %get-tuple-element.14), channel_id=1, replica_groups=mesh['group'=8,'member'=16] {'group','member'}, use_global_device_ids=true, to_apply=%region_17.0 | all-reduce | flops 1 | bytes 8 | tf_op jit(solution)/shard_map/psum | solution.py:89
  656.6 0.6 multiply_reduce_fusion
  657.3 63.6 %all-reduce = (f32[]{:T(128)}, f32[]{:T(128)}) all-reduce(f32[]{:T(128)} %get-tuple-element.3, f32[]{:T(128)} %get-tuple-element.2), channel_id=1, replica_groups=mesh['group'=8,'member'=16] {'group','member'}, use_global_device_ids=true, to_apply=%region_15.0 | all-reduce | flops 2 | bytes 16 | tf_op jit(solution)/shard_map/psum | solution.py:89
  722.2 0.6 multiply_subtract_fusion
  (49 shorter events, 0.4 us)
Async XLA Ops:
  0.6 85.4 %copy-start = (bf16[8,32,256]{2,1,0:T(8,128)(2,1)S(1)}, bf16[8,32,256]{2,1,0:T(8,128)(2,1)}, u32[]{:S(2)}) copy-start(bf16[8,32,256]{2,1,0:T(8,128)(2,1)} %param.18) | copy-start | bytes 393220
  0.6 83.3 %copy-start.2 = (bf16[8,27,1024]{2,0,1:T(8,128)(2,1)S(1)}, bf16[8,27,1024]{2,0,1:T(8,128)(2,1)}, u32[]{:S(2)}) copy-start(bf16[8,27,1024]{2,0,1:T(8,128)(2,1)} %param.19) | copy-start | bytes 1327108
  21.9 64.3 %collective-permute-start.1 = (bf16[128,256]{1,0:T(8,128)(2,1)S(1)}, bf16[128,256]{1,0:T(8,128)(2,1)S(1)}, u32[]{:S(2)}, u32[]{:S(2)}) collective-permute-start(bf16[128,256]{1,0:T(8,128)(2,1)S(1)} %all_gather.18), channel_id=1, source_target_pairs={{16,0},{32,16},{48,32},{64,48},{80,64},{96,80},{112,96},{17,1},{33... | collective-permute-start | bytes 196616 | tf_op jit(solution)/shard_map/ppermute | solution.py:17
  30.0 56.2 %collective-permute-start = (bf16[128,256]{1,0:T(8,128)(2,1)S(1)}, bf16[128,256]{1,0:T(8,128)(2,1)S(1)}, u32[]{:S(2)}, u32[]{:S(2)}) collective-permute-start(bf16[128,256]{1,0:T(8,128)(2,1)S(1)} %all_gather.18), channel_id=1, source_target_pairs={{0,16},{16,32},{32,48},{48,64},{64,80},{80,96},{96,112},{1,17},{17... | collective-permute-start | bytes 196616 | tf_op jit(solution)/shard_map/ppermute | solution.py:16
  84.0 2.0 copy-start.6
  87.0 6.3 copy-start.1
  87.0 6.3 copy-start.3
  87.0 6.3 copy-start.5
  87.0 99.7 %copy-start.7 = (bf16[8,32,256]{2,1,0:T(8,128)(2,1)S(1)}, bf16[8,32,256]{2,1,0:T(8,128)(2,1)}, u32[]{:S(2)}) copy-start(bf16[8,32,256]{2,1,0:T(8,128)(2,1)} %param.17) | copy-start | bytes 393220
  176.7 60.3 %collective-permute-start.3 = (bf16[128,256]{1,0:T(8,128)(2,1)S(1)}, bf16[128,256]{1,0:T(8,128)(2,1)S(1)}, u32[]{:S(2)}, u32[]{:S(2)}) collective-permute-start(bf16[128,256]{1,0:T(8,128)(2,1)S(1)} %all_gather.20), channel_id=1, source_target_pairs={{16,0},{32,16},{48,32},{64,48},{80,64},{96,80},{112,96},{17,1},{33... | collective-permute-start | bytes 196616 | tf_op jit(solution)/shard_map/ppermute | solution.py:17
  184.8 52.2 %collective-permute-start.2 = (bf16[128,256]{1,0:T(8,128)(2,1)S(1)}, bf16[128,256]{1,0:T(8,128)(2,1)S(1)}, u32[]{:S(2)}, u32[]{:S(2)}) collective-permute-start(bf16[128,256]{1,0:T(8,128)(2,1)S(1)} %all_gather.20), channel_id=1, source_target_pairs={{0,16},{16,32},{32,48},{48,64},{64,80},{80,96},{96,112},{1,17},{17... | collective-permute-start | bytes 196616 | tf_op jit(solution)/shard_map/ppermute | solution.py:16
  523.2 60.1 %collective-permute-start.5 = (bf16[128,256]{1,0:T(8,128)(2,1)S(1)}, bf16[128,256]{1,0:T(8,128)(2,1)S(1)}, u32[]{:S(2)}, u32[]{:S(2)}) collective-permute-start(bf16[128,256]{1,0:T(8,128)(2,1)S(1)} %all_gather.22), channel_id=1, source_target_pairs={{16,0},{32,16},{48,32},{64,48},{80,64},{96,80},{112,96},{17,1},{33... | collective-permute-start | bytes 196616 | tf_op jit(solution)/shard_map/ppermute | solution.py:17
  531.1 52.2 %collective-permute-start.4 = (bf16[128,256]{1,0:T(8,128)(2,1)S(1)}, bf16[128,256]{1,0:T(8,128)(2,1)S(1)}, u32[]{:S(2)}, u32[]{:S(2)}) collective-permute-start(bf16[128,256]{1,0:T(8,128)(2,1)S(1)} %all_gather.22), channel_id=1, source_target_pairs={{0,16},{16,32},{32,48},{48,64},{64,80},{80,96},{96,112},{1,17},{17... | collective-permute-start | bytes 196616 | tf_op jit(solution)/shard_map/ppermute | solution.py:16
  584.1 138.2 %copy-start.4 = (f32[2048]{0:T(1024)S(1)}, f32[2048]{0:T(1024)}, u32[]{:S(2)}) copy-start(f32[2048]{0:T(1024)} %param.10) | copy-start | bytes 24580
where the time goes:
time: 724 us; the launch traced here: 723 us
  blocking collectives  645 us (89%)
  starting transfers between devices  30.9 us (4%)
  matrix products  22.1 us (3%)
  between operations  10.2 us (1%)
  other arithmetic  7.66 us (1%)
    psum x4, blocking collectives, shards(): lax.psum((jnp.sum(weight * image), jnp.sum(shifted * direction)), ('group...  256 us
    all_gather x3, blocking collectives, operate(): lax.all_gather(outgoing, ('group', 'member'), axis=0, tiled=True)  143 us
    psum x2, blocking collectives, shards(): lax.psum(jnp.sum(weight * gap), ('group', 'member')) / active_total  128 us
    psum x1, blocking collectives, shards(): norm_now = lax.psum(jnp.sum(shifted * shifted), ('group', 'member'))  63 us
    all_gather x3, blocking collectives, window_of(): whole = lax.all_gather(local_rows, 'member', axis=0, tiled=True)  54.4 us
    ppermute x3, starting transfers between devices, padded(): after = lax.ppermute(leading, axis, down)  24 us
    dot_general x3, matrix products, operate(): jnp.einsum('cnij,cnj->ci', near_blocks, near_rows, preferred_element_type...  18.7 us
  transfers between devices with their start and end apart: 6, of which 0 were waited for; matrix products, arithmetic and copies ran while one was open for 1% of the time, Pallas kernels for 0%

commit v1 on v0

v1 whole, which is shorter than its diff:
```python
import functools

import jax
import jax.numpy as jnp
from jax import lax
from jax.experimental import pallas as pl
from jax.experimental.pallas import tpu as pltpu
from jax.sharding import PartitionSpec as P

MESH = pl.DeviceIdType.MESH
F32 = jnp.float32
BF16 = jnp.bfloat16
GROUPS = 8
MEMBERS = 16
DEVICES = GROUPS * MEMBERS
CL = 8
CS = 256
RANK = 32
NEAR = 9
FAR = 27
WINDOW = 3 * MEMBERS
SCALE = 2.0**-20


def dot(a, b, dims=((1,), (0,))):
    return lax.dot_general(a, b, (dims, ((), ())), preferred_element_type=F32)


def split3(a):
    hi = a.astype(BF16)
    rest = a - hi.astype(F32)
    mid = rest.astype(BF16)
    low = (rest - mid.astype(F32)).astype(BF16)
    return hi, mid, low


def total(a):
    return jnp.sum(jnp.sum(a, axis=0, keepdims=True), axis=1, keepdims=True)


def kernel(
    pressure_hbm,
    height_hbm,
    active_hbm,
    self_hbm,
    near_hbm,
    near_list_hbm,
    far_list_hbm,
    source_hbm,
    target_hbm,
    coupling_hbm,
    pressure_out,
    gap_out,
    pressure_v,
    height_v,
    active_v,
    self_v,
    near_v,
    near_list_v,
    far_list_v,
    source_v,
    target_v,
    coupling_v,
    far_pad,
    near_pick,
    near_dev,
    far_pick,
    far_seg,
    spread,
    fold,
    rows_v,
    couple_v,
    field_out,
    field_in,
    proj0_out,
    proj0_in,
    proj_out,
    proj_in,
    last_out,
    last_in,
    load_sem,
    field_send,
    field_recv,
    proj_send,
    proj_recv,
):
    g = lax.axis_index("group")
    m = lax.axis_index("member")

    def peer(slot):
        return (
            lax.rem(g + lax.div(slot, MEMBERS), GROUPS),
            lax.rem(m + lax.rem(slot, MEMBERS), MEMBERS),
        )

    barrier = pltpu.get_barrier_semaphore()

    def greet(slot, carry):
        pl.semaphore_signal(barrier, inc=1, device_id=peer(slot), device_id_type=MESH)
        return carry

    lax.fori_loop(1, DEVICES, greet, 0)

    pairs = (
        (pressure_hbm, pressure_v),
        (active_hbm, active_v),
        (source_hbm, source_v),
        (near_list_hbm, near_list_v),
        (far_list_hbm, far_list_v),
        (self_hbm, self_v),
        (height_hbm, height_v),
        (coupling_hbm, coupling_v),
        (target_hbm, target_v),
        (near_hbm, near_v),
    )
    loads = [pltpu.make_async_copy(a, b, load_sem.at[i]) for i, (a, b) in enumerate(pairs)]
    for load in loads:
        load.start()

    def wide(ref):
        return jnp.concatenate(
            [ref[pl.ds(0, CL, stride=2), :], ref[pl.ds(1, CL, stride=2), :]], axis=1
        )

    def tall(value):
        return jnp.concatenate([value[:, :128], value[:, 128:]], axis=0)

    row8 = lax.broadcasted_iota(jnp.int32, (CL, CS), 0)
    lane8 = lax.broadcasted_iota(jnp.int32, (CL, CS), 1)
    own = row8 == lax.shift_right_logical(lane8, 5)

    def project(value16):
        product = dot(value16, source_v[...], ((1,), (1,)))
        first = jnp.sum(jnp.where(own, product[:CL], 0.0), axis=0, keepdims=True)
        second = jnp.sum(jnp.where(own, product[CL:], 0.0), axis=0, keepdims=True)
        return first, second

    lane1 = lax.broadcasted_iota(jnp.int32, (1, 128), 1)

    def scalar_row(*values):
        row = jnp.zeros((1, 128), F32)
        for i, value in enumerate(values):
            row = jnp.where(lane1 == i, value, row)
        return row

    def field_copy(phase, slot):
        far_slot = jnp.where(slot >= 2 * MEMBERS, slot + (GROUPS - 3) * MEMBERS, slot)
        return pltpu.make_async_remote_copy(
            src_ref=field_out.at[phase],
            dst_ref=field_in.at[phase, slot],
            send_sem=field_send.at[phase],
            recv_sem=field_recv.at[phase],
            device_id=peer(far_slot),
            device_id_type=MESH,
        )

    def field_all(phase):
        rest = field_in.at[phase, pl.ds(1, WINDOW - 1)]
        return pltpu.make_async_remote_copy(
            src_ref=rest,
            dst_ref=rest,
            send_sem=field_send.at[phase],
            recv_sem=field_recv.at[phase],
            device_id=peer(1),
            device_id_type=MESH,
        )

    def proj_copy(out, into, sem, slot):
        return pltpu.make_async_remote_copy(
            src_ref=out,
            dst_ref=into.at[slot],
            send_sem=proj_send.at[sem],
            recv_sem=proj_recv.at[sem],
            device_id=peer(slot),
            device_id_type=MESH,
        )

    def proj_all(into, sem):
        rest = into.at[pl.ds(1, DEVICES - 1)]
        return pltpu.make_async_remote_copy(
            src_ref=rest,
            dst_ref=rest,
            send_sem=proj_send.at[sem],
            recv_sem=proj_recv.at[sem],
            device_id=peer(1),
            device_id_type=MESH,
        )

    def send_field(phase, value):
        block = tall(value).astype(BF16)
        field_out[phase] = block
        field_in[phase, 0] = block

        def one(slot, carry):
            field_copy(phase, slot).start()
            return carry

        lax.fori_loop(1, WINDOW, one, 0)

    def send_proj(out, into, sem, rows):
        for i, row in enumerate(rows):
            out[i : i + 1, :] = row
            into[0, i : i + 1, :] = row

        def one(slot, carry):
            proj_copy(out, into, sem, slot).start()
            return carry

        lax.fori_loop(1, DEVICES, one, 0)

    loads[0].wait()
    loads[1].wait()
    mask = wide(active_v).astype(F32)
    pressure = wide(pressure_v) * mask
    loads[2].wait()
    first, mask_proj = project(jnp.concatenate([pressure, mask], axis=0).astype(BF16))
    count_own = total(mask)

    pl.semaphore_wait(barrier, DEVICES - 1)
    send_field(0, pressure)
    send_proj(proj0_out, proj0_in, 0, (first[:, :128], first[:, 128:]))
    send_proj(
        proj_out.at[0],
        proj_in.at[0],
        1,
        (mask_proj[:, :128], mask_proj[:, 128:], scalar_row(count_own)),
    )

    loads[3].wait()
    loads[4].wait()
    far_pad[...] = jnp.zeros_like(far_pad)
    far_pad[:, :FAR] = far_list_v[...].astype(F32)
    far_cols = jnp.transpose(far_pad[...])
    near_ids = near_list_v[...]
    dg = lax.bitwise_and(g - lax.shift_right_logical(near_ids, 7), 7)
    dm = lax.bitwise_and(m - lax.bitwise_and(lax.shift_right_logical(near_ids, 3), 15), 15)
    near_slot = jnp.where(dg == 7, 2, dg) * MEMBERS + dm
    near_row = near_slot * (2 * CL) + lax.bitwise_and(near_ids, 7)
    dev_row = dg * MEMBERS + dm
    pick_iota = lax.broadcasted_iota(jnp.int32, (CL, WINDOW * 2 * CL), 1)
    dev_iota = lax.broadcasted_iota(jnp.int32, (CL, DEVICES), 1)
    low, high, dev = [], [], []
    for n in range(NEAR):
        low.append(jnp.where(pick_iota == near_row[:, n : n + 1], 1.0, 0.0))
        high.append(jnp.where(pick_iota == near_row[:, n : n + 1] + CL, 1.0, 0.0))
        dev.append(jnp.where(dev_iota == dev_row[:, n : n + 1], 1.0, 0.0))
    near_pick[...] = jnp.concatenate(low + high, axis=0).astype(BF16)
    near_dev[...] = jnp.concatenate(dev, axis=0).astype(BF16)

    far_ids = far_cols[:RANK, :].astype(jnp.int32)
    fg = lax.bitwise_and(g - lax.shift_right_logical(far_ids, 7), 7)
    fm = lax.bitwise_and(m - lax.bitwise_and(lax.shift_right_logical(far_ids, 3), 15), 15)
    there = lax.broadcasted_iota(jnp.int32, (RANK, CL), 0) < FAR
    far_row = jnp.where(there, fg * MEMBERS + fm, -1)
    far_part = lax.bitwise_and(far_ids, 7)
    far_iota = lax.broadcasted_iota(jnp.int32, (RANK, DEVICES), 1)
    part_iota = lax.shift_right_logical(lax.broadcasted_iota(jnp.int32, (RANK, CS), 1), 5)
    for c in range(CL):
        rows = pl.ds(c * RANK, RANK)
        far_pick[rows, :] = jnp.where(far_iota == far_row[:, c : c + 1], 1.0, 0.0).astype(BF16)
        far_seg[rows, :] = jnp.where(part_iota == far_part[:, c : c + 1], 1.0, 0.0)
    tall_iota = lax.bitwise_and(lax.broadcasted_iota(jnp.int32, (CS, RANK * RANK), 0), RANK - 1)
    wide_iota = lax.bitwise_and(lax.broadcasted_iota(jnp.int32, (CS, RANK * RANK), 1), RANK - 1)
    spread[...] = jnp.where(tall_iota == wide_iota, 1.0, 0.0).astype(BF16)
    tall_iota = lax.shift_right_logical(lax.broadcasted_iota(jnp.int32, (RANK * RANK, CS), 0), 5)
    wide_iota = lax.bitwise_and(lax.broadcasted_iota(jnp.int32, (RANK * RANK, CS), 1), RANK - 1)
    fold[...] = jnp.where(tall_iota == wide_iota, 1.0, 0.0).astype(BF16)
    for load in loads[5:]:
        load.wait()
    compliance = wide(self_v)
    height = wide(height_v)

    row16 = lax.broadcasted_iota(jnp.int32, (2 * CL, CS), 0)

    def gather_field(phase):
        window = field_in[phase].reshape(WINDOW * 2 * CL, 128)
        picked = dot(near_pick[...], window)
        half = NEAR * CL
        return jnp.concatenate([picked[:half], picked[half:]], axis=1)

    def near_sum(rows):
        rows_v[...] = rows

        def cluster(c, acc):
            for n in range(NEAR):
                row = rows_v[pl.ds(n * CL + c, 1), :]
                left = jnp.where(row16 == c, row, 0.0).astype(BF16)
                acc = acc + dot(left, near_v[c, n], ((1,), (1,)))
            return acc

        return lax.fori_loop(0, CL, cluster, jnp.zeros((2 * CL, CS), F32))[:CL]

    def far_sum(projected):
        picked = dot(far_pick[...], projected.astype(BF16))
        spreaded = dot((picked * far_seg[...]).astype(BF16), spread[...])
        for c in range(CL):
            part = spreaded[c * RANK : c * RANK + FAR] * coupling_v[c].astype(F32)
            couple_v[c : c + 1, :] = jnp.sum(part, axis=0, keepdims=True)
        hi, mid, low = split3(couple_v[...])
        coupled = dot(hi, fold[...]) + (dot(mid, fold[...]) + dot(low, fold[...]))
        return dot(jnp.where(own, coupled, 0.0).astype(BF16), target_v[...])

    def operate(value, rows, projected):
        narrow = value.astype(BF16).astype(F32)
        return compliance * narrow + (near_sum(rows) + far_sum(projected))

    def proj_rows(ref):
        return jnp.concatenate([ref[:, 0, :], ref[:, 1, :]], axis=1)

    def near_scalars(scalars):
        hi, mid, low = split3(scalars)
        return dot(near_dev[...], hi) + (dot(near_dev[...], mid) + dot(near_dev[...], low))

    field_all(0).wait_recv()
    proj_all(proj0_in, 0).wait_recv()
    rows0 = gather_field(0)
    mask_rows = jnp.where(rows0 != 0.0, 1.0, 0.0)
    gap = operate(pressure, rows0, proj_rows(proj0_in)) - height

    safe_count = jnp.maximum(count_own, 1.0)
    gap_sum = total(mask * gap)
    gap_centre = gap_sum / safe_count
    local = (gap - gap_centre) * mask
    send_field(1, local)
    zeros = jnp.zeros_like(local)
    first, _ = project(jnp.concatenate([local, zeros], axis=0).astype(BF16))
    send_proj(
        proj_out.at[1],
        proj_in.at[1],
        2,
        (first[:, :128], first[:, 128:], scalar_row(gap_sum, gap_centre)),
    )

    proj_all(proj_in.at[0], 1).wait_recv()
    mask_projs = proj_rows(proj_in.at[0])
    counts = proj_in[0, :, 2, :][:, 0:1]
    count = jnp.sum(counts, axis=0, keepdims=True)

    field_all(1).wait_recv()
    proj_all(proj_in.at[1], 2).wait_recv()
    scalars = proj_in[1, :, 2, :]
    gap_mean = jnp.sum(scalars[:, 0:1], axis=0, keepdims=True) / count
    direction = (gap - gap_mean) * mask
    here = near_scalars(scalars)
    rows1 = gather_field(1) + (here[:, 1:2] - gap_mean) * mask_rows
    projs1 = proj_rows(proj_in.at[1]) + (scalars[:, 1:2] - gap_mean) * mask_projs
    image = operate(direction, rows1, projs1)

    image_sum = total(mask * image)
    image_centre = image_sum / safe_count
    centred = (image - image_centre) * mask
    norm_own = total(direction * direction)
    fit = total(centred * direction) / jnp.where(norm_own > 0.0, norm_own, 1.0)
    local = centred - fit * direction
    send_field(2, local)
    first, _ = project(jnp.concatenate([local, zeros], axis=0).astype(BF16))
    small = centred * SCALE
    send_proj(
        proj_out.at[2],
        proj_in.at[2],
        3,
        (
            first[:, :128],
            first[:, 128:],
            scalar_row(
                image_sum,
                total(mask * image * direction),
                total(mask * direction),
                norm_own,
                total(small * small),
                image_centre,
                fit,
            ),
        ),
    )

    field_all(2).wait_recv()
    proj_all(proj_in.at[2], 3).wait_recv()
    scalars = proj_in[2, :, 2, :]
    sums = jnp.sum(scalars, axis=0, keepdims=True)
    image_mean = sums[:, 0:1] / count
    norm_old = sums[:, 3:4]
    step = norm_old / (sums[:, 1:2] - image_mean * sums[:, 2:3])
    shifts = scalars[:, 5:6] - image_mean
    small_shifts = shifts * SCALE
    spread_sum = sums[:, 4:5] + jnp.sum(
        counts * (small_shifts * small_shifts), axis=0, keepdims=True
    )
    long_step = step / SCALE
    norm_now = long_step * (long_step * spread_sum) - norm_old
    ratio = norm_now / norm_old
    pressure = pressure - step * direction
    gap = gap - step * image
    shifted = (gap - (gap_mean - step * image_mean)) * mask
    previous = direction
    direction = shifted + ratio * previous
    here = near_scalars(scalars)
    rows2 = (
        (1.0 + ratio - step * here[:, 6:7]) * rows1
        - step * gather_field(2)
        - step * (here[:, 5:6] - image_mean) * mask_rows
    )
    projs2 = (
        (1.0 + ratio - step * scalars[:, 6:7]) * projs1
        - step * proj_rows(proj_in.at[2])
        - step * shifts * mask_projs
    )
    image = operate(direction, rows2, projs2)

    send_proj(
        last_out,
        last_in,
        4,
        (
            scalar_row(
                total(mask * image),
                total(mask * image * direction),
                total(mask * direction),
                total(shifted * direction),
            ),
        ),
    )
    proj_all(last_in, 4).wait_recv()
    sums = jnp.sum(last_in[:, 0, :], axis=0, keepdims=True)
    image_mean = sums[:, 0:1] / count
    step = sums[:, 3:4] / (sums[:, 1:2] - image_mean * sums[:, 2:3])
    pressure = pressure - step * direction
    gap = gap - step * image
    for ref, value in ((pressure_out, pressure), (gap_out, gap)):
        ref[pl.ds(0, CL, stride=2), :] = value[:, :128]
        ref[pl.ds(1, CL, stride=2), :] = value[:, 128:]

    for phase in range(3):
        field_all(phase).wait_send()
    proj_all(proj0_in, 0).wait_send()
    for i in range(3):
        proj_all(proj_in.at[i], i + 1).wait_send()
    proj_all(last_in, 4).wait_send()


def shards(
    pressure_init,
    gap_height,
    active,
    self_compliance,
    near_blocks,
    near_list,
    far_list,
    source_basis,
    target_basis,
    coupling,
):
    elements = pressure_init.shape[0]
    fold_shape = (elements // 128, 128)
    vmem = pltpu.VMEM
    scratch = [
        vmem(fold_shape, F32),
        vmem(fold_shape, F32),
        vmem(fold_shape, jnp.int32),
        vmem(fold_shape, F32),
        vmem((CL, NEAR, CS, CS), BF16),
        vmem((CL, NEAR), jnp.int32),
        vmem((CL, FAR), jnp.int32),
        vmem((CL * RANK, CS), BF16),
        vmem((CL * RANK, CS), BF16),
        vmem((CL, FAR, RANK * RANK), BF16),
        vmem((CL, 128), F32),
        vmem((2 * NEAR * CL, WINDOW * 2 * CL), BF16),
        vmem((NEAR * CL, DEVICES), BF16),
        vmem((CL * RANK, DEVICES), BF16),
        vmem((CL * RANK, CS), F32),
        vmem((CS, RANK * RANK), BF16),
        vmem((RANK * RANK, CS), BF16),
        vmem((NEAR * CL, CS), F32),
        vmem((CL, RANK * RANK), F32),
        vmem((3, 2 * CL, 128), BF16),
        vmem((3, WINDOW, 2 * CL, 128), BF16),
        vmem((2, 128), F32),
        vmem((DEVICES, 2, 128), F32),
        vmem((3, 3, 128), F32),
        vmem((3, DEVICES, 3, 128), F32),
        vmem((1, 128), F32),
        vmem((DEVICES, 1, 128), F32),
        pltpu.SemaphoreType.DMA((10,)),
        pltpu.SemaphoreType.DMA((3,)),
        pltpu.SemaphoreType.DMA((3,)),
        pltpu.SemaphoreType.DMA((5,)),
        pltpu.SemaphoreType.DMA((5,)),
    ]
    pressure, gap = pl.pallas_call(
        kernel,
        out_shape=[jax.ShapeDtypeStruct(fold_shape, F32)] * 2,
        in_specs=[pl.BlockSpec(memory_space=pl.ANY)] * 10,
        out_specs=[pl.BlockSpec(memory_space=pltpu.VMEM)] * 2,
        scratch_shapes=scratch,
        compiler_params=pltpu.CompilerParams(
            collective_id=0, has_side_effects=True, vmem_limit_bytes=40 * 2**20
        ),
    )(
        pressure_init.reshape(fold_shape),
        gap_height.reshape(fold_shape),
        active.reshape(fold_shape),
        self_compliance.reshape(fold_shape),
        near_blocks,
        near_list,
        far_list,
        source_basis.reshape(CL * RANK, CS),
        target_basis.reshape(CL * RANK, CS),
        coupling,
    )
    return pressure.reshape(elements), gap.reshape(elements)


def solution(mesh):
    spec = P(("group", "member"))
    return jax.shard_map(
        shards, mesh=mesh, in_specs=(spec,) * 10, out_specs=(spec, spec), check_vma=False
    )
```

time: 724 us -> 72.4 us (0.10)
  blocking collectives: 645 us -> 0 us
  Pallas kernels: 0 us -> 59.2 us
  starting transfers between devices: 30.9 us -> 0 us
  matrix products: 22.1 us -> 0 us
  between operations: 10.2 us -> 0.66 us
  other arithmetic: 7.66 us -> 0 us
    psum x7 -> x0, blocking collectives: 447 us -> none  [the longest x4 256 us: shards(): lax.psum((jnp.sum(weight * image), jnp.sum(shifted * direction)), ('group...]
    all_gather x6 -> x0, blocking collectives: 198 us -> none  [the longest x3 143 us: operate(): lax.all_gather(outgoing, ('group', 'member'), axis=0, tiled=True)]
    pallas_call x0 -> x1, Pallas kernels: none -> 59.2 us  [shards(): pl.pallas_call(kernel, out_shape=[jax.ShapeDtypeStruct(fold_shape, F32)]...]
    ppermute x6 -> x0, starting transfers between devices: 30.9 us -> none  [the longest x3 24 us: padded(): after = lax.ppermute(leading, axis, down)]
    dot_general x12 -> x0, matrix products: 22.1 us -> none  [the longest x3 18.7 us: operate(): jnp.einsum('cnij,cnj->ci', near_blocks, near_rows, preferred_element_type...]
    unnamed x22 -> x21, local copies, waits for them, and re-layouts: 0.36 us -> 12.1 us
  transfers between devices with their start and end apart: 6 -> 0, of which waited for: 0 -> 0; matrix products, arithmetic and copies ran while one was open for 1% -> 0% of each run, Pallas kernels for 0% -> 0%
where the time goes in v1:
time: 72.4 us; the launch traced here: 71.9 us
  Pallas kernels  59.2 us (82%)
  local copies, waits for them, and re-layouts  12.1 us (17%)
    pallas_call x1, Pallas kernels, shards(): pl.pallas_call(kernel, out_shape=[jax.ShapeDtypeStruct(fold_shape, F32)]...  59.2 us
    unnamed x21, local copies, waits for them, and re-layouts  12.1 us

profile of v1, /device:TPU:1, one launch (start us, length us, event | category | flops | bytes accessed | tf_op | source)
XLA Modules:
  0.0 71.9 jit_solution(7104031890650596371)
XLA Ops:
  0.6 1.3 %copy.12.coupling_hbm = bf16[8,27,1024]{2,1,0:T(8,128)(2,1)S(1)} copy(bf16[8,27,1024]{2,0,1:T(8,128)(2,1)} %param.19) | data formatting | bytes 884736 | tf_op args[9]
  1.9 0.0 copy-start
  1.9 3.7 %copy-done = bf16[8,9,256,256]{3,2,1,0:T(8,128)(2,1)S(1)} copy-done((bf16[8,9,256,256]{3,2,1,0:T(8,128)(2,1)S(1)}, bf16[8,9,256,256]{3,2,1,0:T(8,128)(2,1)}, u32[]{:S(2)}) %copy-start) | copy-done | bytes 9437208
  5.6 0.0 copy-start.1
  5.6 0.9 %copy-done.1 = bf16[8,32,256]{2,1,0:T(8,128)(2,1)S(1)} copy-done((bf16[8,32,256]{2,1,0:T(8,128)(2,1)S(1)}, bf16[8,32,256]{2,1,0:T(8,128)(2,1)}, u32[]{:S(2)}) %copy-start.1) | copy-done | bytes 131096
  6.5 0.0 copy-start.2
  6.5 0.9 %copy-done.2 = bf16[8,32,256]{2,1,0:T(8,128)(2,1)S(1)} copy-done((bf16[8,32,256]{2,1,0:T(8,128)(2,1)S(1)}, bf16[8,32,256]{2,1,0:T(8,128)(2,1)}, u32[]{:S(2)}) %copy-start.2) | copy-done | bytes 131096
  7.4 0.0 copy-start.3
  7.4 0.7 copy-done.3
  8.1 0.0 copy-start.4
  8.1 0.7 copy-done.4
  8.8 0.0 copy-start.5
  8.8 0.7 copy-done.5
  9.5 0.0 copy-start.6
  9.5 0.7 copy-done.6
  10.2 0.0 copy-start.7
  10.2 0.7 copy-done.7
  10.9 0.0 copy-start.8
  10.9 0.7 copy-done.8
  11.6 59.2 %shard_map.113 = (f32[16,128]{1,0:T(8,128)S(1)}, f32[16,128]{1,0:T(8,128)S(1)}) custom-call(f32[16,128]{1,0:T(8,128)S(1)} %bitcast.12, f32[16,128]{1,0:T(8,128)S(1)} %bitcast.13, s32[16,128]{1,0:T(8,128)S(1)} %bitcast.14, f32[16,128]{1,0:T(8,128)S(1)} %bitcast.15, bf16[8,9,256,256]{3,2,1,0:T(8,128)(2,1)S(1)} %copy-done, s32[8,9]{1,0:T(8,128)S(1)} %copy-done.7, ...), custom_call_target="tpu_custom_call" | custom-call | tf_op jit(solution)/shard_map/pallas_call | solution.py:490
  70.7 0.6 copy.15
  71.3 0.6 copy.16
Async XLA Ops:
  1.9 3.7 %copy-start = (bf16[8,9,256,256]{3,2,1,0:T(8,128)(2,1)S(1)}, bf16[8,9,256,256]{3,2,1,0:T(8,128)(2,1)}, u32[]{:S(2)}) copy-start(bf16[8,9,256,256]{3,2,1,0:T(8,128)(2,1)} %near_hbm.1) | copy-start | bytes 28311556
  5.6 0.9 %copy-start.1 = (bf16[8,32,256]{2,1,0:T(8,128)(2,1)S(1)}, bf16[8,32,256]{2,1,0:T(8,128)(2,1)}, u32[]{:S(2)}) copy-start(bf16[8,32,256]{2,1,0:T(8,128)(2,1)} %param.17) | copy-start | bytes 393220
  6.5 0.9 %copy-start.2 = (bf16[8,32,256]{2,1,0:T(8,128)(2,1)S(1)}, bf16[8,32,256]{2,1,0:T(8,128)(2,1)}, u32[]{:S(2)}) copy-start(bf16[8,32,256]{2,1,0:T(8,128)(2,1)} %param.18) | copy-start | bytes 393220
  7.4 0.7 copy-start.3
  8.1 0.7 copy-start.4
  8.8 0.7 copy-start.5
  9.5 0.7 copy-start.6
  10.2 0.7 copy-start.7
  10.9 0.7 copy-start.8

commit v2 on v1

--- a/solution.py
+++ b/solution.py
@@ -20,6 +20,15 @@
 FAR = 27
 WINDOW = 3 * MEMBERS
 SCALE = 2.0**-20
+
+
+def hops(slot):
+    steps = (slot & 3, slot >> 2 & 3, slot >> 5)
+    return sum(min(step, 4 - step) for step in steps)
+
+
+FAR_FIRST = sorted(range(1, DEVICES), key=lambda slot: -hops(slot))
+FIELD_FIRST = sorted(range(1, WINDOW), key=lambda slot: -hops(slot % MEMBERS))
 
 
 def dot(a, b, dims=((1,), (0,))):
@@ -87,19 +96,20 @@
     g = lax.axis_index("group")
     m = lax.axis_index("member")
 
+    def around(dy, dz):
+        return lax.bitwise_and(m + 4 * dy, 12) + lax.bitwise_and(m + dz, 3)
+
+    groups = [lax.bitwise_and(g + 2 * dx, 6) + lax.bitwise_xor(lax.bitwise_and(g, 1), dc) for dx in range(4) for dc in range(2)]
+    members = [around(dy, dz) for dy in range(4) for dz in range(4)]
+    sides = (g, lax.bitwise_and(g + 1, 7), lax.bitwise_and(g + 7, 7))
+
     def peer(slot):
-        return (
-            lax.rem(g + lax.div(slot, MEMBERS), GROUPS),
-            lax.rem(m + lax.rem(slot, MEMBERS), MEMBERS),
-        )
+        return groups[slot // MEMBERS], members[slot % MEMBERS]
 
     barrier = pltpu.get_barrier_semaphore()
 
-    def greet(slot, carry):
+    for slot in FAR_FIRST:
         pl.semaphore_signal(barrier, inc=1, device_id=peer(slot), device_id_type=MESH)
-        return carry
-
-    lax.fori_loop(1, DEVICES, greet, 0)
 
     pairs = (
         (pressure_hbm, pressure_v),
@@ -144,13 +154,12 @@
         return row
 
     def field_copy(phase, slot):
-        far_slot = jnp.where(slot >= 2 * MEMBERS, slot + (GROUPS - 3) * MEMBERS, slot)
         return pltpu.make_async_remote_copy(
             src_ref=field_out.at[phase],
             dst_ref=field_in.at[phase, slot],
             send_sem=field_send.at[phase],
             recv_sem=field_recv.at[phase],
-            device_id=peer(far_slot),
+            device_id=(sides[slot // MEMBERS], members[slot % MEMBERS]),
             device_id_type=MESH,
         )
 
@@ -190,23 +199,15 @@
         block = tall(value).astype(BF16)
         field_out[phase] = block
         field_in[phase, 0] = block
-
-        def one(slot, carry):
+        for slot in FIELD_FIRST:
             field_copy(phase, slot).start()
-            return carry
-
-        lax.fori_loop(1, WINDOW, one, 0)
 
     def send_proj(out, into, sem, rows):
         for i, row in enumerate(rows):
             out[i : i + 1, :] = row
             into[0, i : i + 1, :] = row
-
-        def one(slot, carry):
+        for slot in FAR_FIRST:
             proj_copy(out, into, sem, slot).start()
-            return carry
-
-        lax.fori_loop(1, DEVICES, one, 0)
 
     loads[0].wait()
     loads[1].wait()
@@ -216,27 +217,26 @@
     first, mask_proj = project(jnp.concatenate([pressure, mask], axis=0).astype(BF16))
     count_own = total(mask)
 
-    pl.semaphore_wait(barrier, DEVICES - 1)
-    send_field(0, pressure)
-    send_proj(proj0_out, proj0_in, 0, (first[:, :128], first[:, 128:]))
-    send_proj(
-        proj_out.at[0],
-        proj_in.at[0],
-        1,
-        (mask_proj[:, :128], mask_proj[:, 128:], scalar_row(count_own)),
-    )
-
     loads[3].wait()
     loads[4].wait()
     far_pad[...] = jnp.zeros_like(far_pad)
     far_pad[:, :FAR] = far_list_v[...].astype(F32)
     far_cols = jnp.transpose(far_pad[...])
     near_ids = near_list_v[...]
+
+    def member_part(ids):
+        dy = lax.bitwise_and(m - lax.bitwise_and(lax.shift_right_logical(ids, 3), 12), 12)
+        return dy + lax.bitwise_and(m - lax.shift_right_logical(ids, 3), 3)
+
+    def group_part(ids):
+        theirs = lax.shift_right_logical(ids, 7)
+        dx = lax.bitwise_and(g - lax.bitwise_and(theirs, 6), 6)
+        return (dx + lax.bitwise_and(g + theirs, 1)) * MEMBERS
+
     dg = lax.bitwise_and(g - lax.shift_right_logical(near_ids, 7), 7)
-    dm = lax.bitwise_and(m - lax.bitwise_and(lax.shift_right_logical(near_ids, 3), 15), 15)
-    near_slot = jnp.where(dg == 7, 2, dg) * MEMBERS + dm
+    near_slot = jnp.where(dg == 7, 2, dg) * MEMBERS + member_part(near_ids)
     near_row = near_slot * (2 * CL) + lax.bitwise_and(near_ids, 7)
-    dev_row = dg * MEMBERS + dm
+    dev_row = group_part(near_ids) + member_part(near_ids)
     pick_iota = lax.broadcasted_iota(jnp.int32, (CL, WINDOW * 2 * CL), 1)
     dev_iota = lax.broadcasted_iota(jnp.int32, (CL, DEVICES), 1)
     low, high, dev = [], [], []
@@ -248,10 +248,8 @@
     near_dev[...] = jnp.concatenate(dev, axis=0).astype(BF16)
 
     far_ids = far_cols[:RANK, :].astype(jnp.int32)
-    fg = lax.bitwise_and(g - lax.shift_right_logical(far_ids, 7), 7)
-    fm = lax.bitwise_and(m - lax.bitwise_and(lax.shift_right_logical(far_ids, 3), 15), 15)
     there = lax.broadcasted_iota(jnp.int32, (RANK, CL), 0) < FAR
-    far_row = jnp.where(there, fg * MEMBERS + fm, -1)
+    far_row = jnp.where(there, group_part(far_ids) + member_part(far_ids), -1)
     far_part = lax.bitwise_and(far_ids, 7)
     far_iota = lax.broadcasted_iota(jnp.int32, (RANK, DEVICES), 1)
     part_iota = lax.shift_right_logical(lax.broadcasted_iota(jnp.int32, (RANK, CS), 1), 5)
@@ -265,10 +263,27 @@
     tall_iota = lax.shift_right_logical(lax.broadcasted_iota(jnp.int32, (RANK * RANK, CS), 0), 5)
     wide_iota = lax.bitwise_and(lax.broadcasted_iota(jnp.int32, (RANK * RANK, CS), 1), RANK - 1)
     fold[...] = jnp.where(tall_iota == wide_iota, 1.0, 0.0).astype(BF16)
+    pl.semaphore_wait(barrier, DEVICES - 1)
+    send_field(0, pressure)
+    send_proj(proj0_out, proj0_in, 0, (first[:, :128], first[:, 128:]))
+    send_proj(
+        proj_out.at[0],
+        proj_in.at[0],
+        1,
+        (mask_proj[:, :128], mask_proj[:, 128:], scalar_row(count_own)),
+    )
+
     for load in loads[5:]:
         load.wait()
     compliance = wide(self_v)
     height = wide(height_v)
+
+    def turn(c, carry):
+        for n in range(NEAR):
+            near_v[c, n] = jnp.transpose(near_v[c, n])
+        return carry
+
+    lax.fori_loop(0, CL, turn, 0)
 
     row16 = lax.broadcasted_iota(jnp.int32, (2 * CL, CS), 0)
 
@@ -281,14 +296,13 @@
     def near_sum(rows):
         rows_v[...] = rows
 
-        def cluster(c, acc):
+        acc = jnp.zeros((2 * CL, CS), F32)
+        for c in range(CL):
             for n in range(NEAR):
-                row = rows_v[pl.ds(n * CL + c, 1), :]
+                row = rows_v[n * CL + c : n * CL + c + 1, :]
                 left = jnp.where(row16 == c, row, 0.0).astype(BF16)
-                acc = acc + dot(left, near_v[c, n], ((1,), (1,)))
-            return acc
-
-        return lax.fori_loop(0, CL, cluster, jnp.zeros((2 * CL, CS), F32))[:CL]
+                acc = acc + dot(left, near_v[c, n])
+        return acc[:CL]
 
     def far_sum(projected):
         picked = dot(far_pick[...], projected.astype(BF16))
@@ -494,7 +508,7 @@
         out_specs=[pl.BlockSpec(memory_space=pltpu.VMEM)] * 2,
         scratch_shapes=scratch,
         compiler_params=pltpu.CompilerParams(
-            collective_id=0, has_side_effects=True, vmem_limit_bytes=40 * 2**20
+            collective_id=0, has_side_effects=True, vmem_limit_bytes=60 * 2**20
         ),
     )(
         pressure_init.reshape(fold_shape),

time: 72.4 us -> 55.6 us (0.77)
  Pallas kernels: 59.2 us -> 50.1 us
  local copies, waits for them, and re-layouts: 12.1 us -> 4.64 us
    pallas_call x1, Pallas kernels: 59.2 us -> 50.1 us  [shards(): pl.pallas_call(kernel, out_shape=[jax.ShapeDtypeStruct(fold_shape, F32)]...]
    unnamed x21 -> x3, local copies, waits for them, and re-layouts: 12.1 us -> 4.64 us
where the time goes in v2:
time: 55.6 us; the launch traced here: 55.3 us
  Pallas kernels  50.1 us (90%)
  local copies, waits for them, and re-layouts  4.64 us (8%)
  between operations  0.64 us (1%)
    pallas_call x1, Pallas kernels, shards(): pl.pallas_call(kernel, out_shape=[jax.ShapeDtypeStruct(fold_shape, F32)]...  50.1 us
    unnamed x3, local copies, waits for them, and re-layouts  4.64 us

profile of v2, /device:TPU:1, one launch (start us, length us, event | category | flops | bytes accessed | tf_op | source)
XLA Modules:
  0.0 55.3 jit_solution(3416409847304127427)
XLA Ops:
  0.6 2.1 %copy.12.coupling_hbm = bf16[8,27,1024]{2,1,0:T(8,128)(2,1)} copy(bf16[8,27,1024]{2,0,1:T(8,128)(2,1)} %param.19) | data formatting | bytes 884736 | tf_op args[9]
  2.7 50.1 %shard_map.113 = (f32[16,128]{1,0:T(8,128)}, f32[16,128]{1,0:T(8,128)}) custom-call(f32[16,128]{1,0:T(8,128)} %bitcast.12, f32[16,128]{1,0:T(8,128)} %bitcast.13, s32[16,128]{1,0:T(8,128)} %bitcast.14, f32[16,128]{1,0:T(8,128)} %bitcast.15, bf16[8,9,256,256]{3,2,1,0:T(8,128)(2,1)} %near_hbm.1, s32[8,9]{1,0:T(8,128)} %near_list_hbm.1, s32[8,27]{1,0:T(8,128)} %far_list_hbm.1, ...), custom_call_target="tpu_custom_call" | custom-call | tf_op jit(solution)/shard_map/pallas_call | solution.py:504
  52.8 1.3 %copy.15 = f32[2048]{0:T(1024)} copy(f32[2048]{0:T(1024)} %bitcast.11) | data formatting | bytes 16384
  54.0 1.3 %copy.16 = f32[2048]{0:T(1024)} copy(f32[2048]{0:T(1024)} %bitcast.10) | data formatting | bytes 16384

commit v3 on v2

--- a/solution.py
+++ b/solution.py
@@ -60,6 +60,9 @@
     coupling_hbm,
     pressure_out,
     gap_out,
+    direction_out,
+    image_out,
+    step_out,
     pressure_v,
     height_v,
     active_v,
@@ -70,7 +73,6 @@
     source_v,
     target_v,
     coupling_v,
-    far_pad,
     near_pick,
     near_dev,
     far_pick,
@@ -78,7 +80,6 @@
     spread,
     fold,
     rows_v,
-    couple_v,
     field_out,
     field_in,
     proj0_out,
@@ -219,9 +220,6 @@
 
     loads[3].wait()
     loads[4].wait()
-    far_pad[...] = jnp.zeros_like(far_pad)
-    far_pad[:, :FAR] = far_list_v[...].astype(F32)
-    far_cols = jnp.transpose(far_pad[...])
     near_ids = near_list_v[...]
 
     def member_part(ids):
@@ -247,16 +245,16 @@
     near_pick[...] = jnp.concatenate(low + high, axis=0).astype(BF16)
     near_dev[...] = jnp.concatenate(dev, axis=0).astype(BF16)
 
-    far_ids = far_cols[:RANK, :].astype(jnp.int32)
-    there = lax.broadcasted_iota(jnp.int32, (RANK, CL), 0) < FAR
-    far_row = jnp.where(there, group_part(far_ids) + member_part(far_ids), -1)
+    far_ids = far_list_v[...]
+    far_row = group_part(far_ids) + member_part(far_ids)
     far_part = lax.bitwise_and(far_ids, 7)
-    far_iota = lax.broadcasted_iota(jnp.int32, (RANK, DEVICES), 1)
-    part_iota = lax.shift_right_logical(lax.broadcasted_iota(jnp.int32, (RANK, CS), 1), 5)
-    for c in range(CL):
-        rows = pl.ds(c * RANK, RANK)
-        far_pick[rows, :] = jnp.where(far_iota == far_row[:, c : c + 1], 1.0, 0.0).astype(BF16)
-        far_seg[rows, :] = jnp.where(part_iota == far_part[:, c : c + 1], 1.0, 0.0)
+    part_iota = lax.shift_right_logical(lane8, 5)
+    picks, parts = [], []
+    for f in range(FAR):
+        picks.append(jnp.where(dev_iota == far_row[:, f : f + 1], 1.0, 0.0))
+        parts.append(jnp.where(part_iota == far_part[:, f : f + 1], 1.0, 0.0))
+    far_pick[...] = jnp.concatenate(picks, axis=0).astype(BF16)
+    far_seg[...] = jnp.concatenate(parts, axis=0)
     tall_iota = lax.bitwise_and(lax.broadcasted_iota(jnp.int32, (CS, RANK * RANK), 0), RANK - 1)
     wide_iota = lax.bitwise_and(lax.broadcasted_iota(jnp.int32, (CS, RANK * RANK), 1), RANK - 1)
     spread[...] = jnp.where(tall_iota == wide_iota, 1.0, 0.0).astype(BF16)
@@ -293,30 +291,37 @@
         half = NEAR * CL
         return jnp.concatenate([picked[:half], picked[half:]], axis=1)
 
-    def near_sum(rows):
+    def near_products(rows):
         rows_v[...] = rows
-
-        acc = jnp.zeros((2 * CL, CS), F32)
-        for c in range(CL):
-            for n in range(NEAR):
+        products = []
+        for n in range(NEAR):
+            acc = jnp.zeros((2 * CL, CS), F32)
+            for c in range(CL):
                 row = rows_v[n * CL + c : n * CL + c + 1, :]
                 left = jnp.where(row16 == c, row, 0.0).astype(BF16)
                 acc = acc + dot(left, near_v[c, n])
-        return acc[:CL]
+            products.append(acc[:CL])
+        return jnp.concatenate(products, axis=0)
+
+    def slot_sum(products):
+        out = products[:CL]
+        for n in range(1, NEAR):
+            out = out + products[n * CL : (n + 1) * CL]
+        return out
 
     def far_sum(projected):
         picked = dot(far_pick[...], projected.astype(BF16))
         spreaded = dot((picked * far_seg[...]).astype(BF16), spread[...])
-        for c in range(CL):
-            part = spreaded[c * RANK : c * RANK + FAR] * coupling_v[c].astype(F32)
-            couple_v[c : c + 1, :] = jnp.sum(part, axis=0, keepdims=True)
-        hi, mid, low = split3(couple_v[...])
+        summed = jnp.zeros((CL, RANK * RANK), F32)
+        for f in range(FAR):
+            summed = summed + spreaded[f * CL : (f + 1) * CL] * coupling_v[f].astype(F32)
+        hi, mid, low = split3(summed)
         coupled = dot(hi, fold[...]) + (dot(mid, fold[...]) + dot(low, fold[...]))
         return dot(jnp.where(own, coupled, 0.0).astype(BF16), target_v[...])
 
-    def operate(value, rows, projected):
+    def operate(value, products, projected):
         narrow = value.astype(BF16).astype(F32)
-        return compliance * narrow + (near_sum(rows) + far_sum(projected))
+        return compliance * narrow + (slot_sum(products) + far_sum(projected))
 
     def proj_rows(ref):
         return jnp.concatenate([ref[:, 0, :], ref[:, 1, :]], axis=1)
@@ -326,10 +331,11 @@
         return dot(near_dev[...], hi) + (dot(near_dev[...], mid) + dot(near_dev[...], low))
 
     field_all(0).wait_recv()
-    proj_all(proj0_in, 0).wait_recv()
     rows0 = gather_field(0)
     mask_rows = jnp.where(rows0 != 0.0, 1.0, 0.0)
-    gap = operate(pressure, rows0, proj_rows(proj0_in)) - height
+    near0 = near_products(rows0)
+    proj_all(proj0_in, 0).wait_recv()
+    gap = operate(pressure, near0, proj_rows(proj0_in)) - height
 
     safe_count = jnp.maximum(count_own, 1.0)
     gap_sum = total(mask * gap)
@@ -345,20 +351,22 @@
         (first[:, :128], first[:, 128:], scalar_row(gap_sum, gap_centre)),
     )
 
+    mask_near = near_products(mask_rows)
     proj_all(proj_in.at[0], 1).wait_recv()
     mask_projs = proj_rows(proj_in.at[0])
     counts = proj_in[0, :, 2, :][:, 0:1]
     count = jnp.sum(counts, axis=0, keepdims=True)
 
     field_all(1).wait_recv()
+    near1 = near_products(gather_field(1))
     proj_all(proj_in.at[1], 2).wait_recv()
     scalars = proj_in[1, :, 2, :]
     gap_mean = jnp.sum(scalars[:, 0:1], axis=0, keepdims=True) / count
     direction = (gap - gap_mean) * mask
     here = near_scalars(scalars)
-    rows1 = gather_field(1) + (here[:, 1:2] - gap_mean) * mask_rows
+    near1 = near1 + (here[:, 1:2] - gap_mean) * mask_near
     projs1 = proj_rows(proj_in.at[1]) + (scalars[:, 1:2] - gap_mean) * mask_projs
-    image = operate(direction, rows1, projs1)
+    image = operate(direction, near1, projs1)
 
     image_sum = total(mask * image)
     image_centre = image_sum / safe_count
@@ -389,6 +397,7 @@
     )
 
     field_all(2).wait_recv()
+    near2 = near_products(gather_field(2))
     proj_all(proj_in.at[2], 3).wait_recv()
     scalars = proj_in[2, :, 2, :]
     sums = jnp.sum(scalars, axis=0, keepdims=True)
@@ -409,17 +418,26 @@
     previous = direction
     direction = shifted + ratio * previous
     here = near_scalars(scalars)
-    rows2 = (
-        (1.0 + ratio - step * here[:, 6:7]) * rows1
-        - step * gather_field(2)
-        - step * (here[:, 5:6] - image_mean) * mask_rows
+    near2 = (
+        (1.0 + ratio - step * here[:, 6:7]) * near1
+        - step * near2
+        - step * (here[:, 5:6] - image_mean) * mask_near
     )
     projs2 = (
         (1.0 + ratio - step * scalars[:, 6:7]) * projs1
         - step * proj_rows(proj_in.at[2])
         - step * shifts * mask_projs
     )
-    image = operate(direction, rows2, projs2)
+    image = operate(direction, near2, projs2)
+
+    for ref, value in (
+        (pressure_out, pressure),
+        (gap_out, gap),
+        (direction_out, direction),
+        (image_out, image),
+    ):
+        ref[pl.ds(0, CL, stride=2), :] = value[:, :128]
+        ref[pl.ds(1, CL, stride=2), :] = value[:, 128:]
 
     send_proj(
         last_out,
@@ -438,11 +456,7 @@
     sums = jnp.sum(last_in[:, 0, :], axis=0, keepdims=True)
     image_mean = sums[:, 0:1] / count
     step = sums[:, 3:4] / (sums[:, 1:2] - image_mean * sums[:, 2:3])
-    pressure = pressure - step * direction
-    gap = gap - step * image
-    for ref, value in ((pressure_out, pressure), (gap_out, gap)):
-        ref[pl.ds(0, CL, stride=2), :] = value[:, :128]
-        ref[pl.ds(1, CL, stride=2), :] = value[:, 128:]
+    step_out[...] = jnp.broadcast_to(step, step_out.shape)
 
     for phase in range(3):
         field_all(phase).wait_send()
@@ -477,16 +491,14 @@
         vmem((CL, FAR), jnp.int32),
         vmem((CL * RANK, CS), BF16),
         vmem((CL * RANK, CS), BF16),
-        vmem((CL, FAR, RANK * RANK), BF16),
-        vmem((CL, 128), F32),
+        vmem((FAR, CL, RANK * RANK), BF16),
         vmem((2 * NEAR * CL, WINDOW * 2 * CL), BF16),
         vmem((NEAR * CL, DEVICES), BF16),
-        vmem((CL * RANK, DEVICES), BF16),
-        vmem((CL * RANK, CS), F32),
+        vmem((FAR * CL, DEVICES), BF16),
+        vmem((FAR * CL, CS), F32),
         vmem((CS, RANK * RANK), BF16),
         vmem((RANK * RANK, CS), BF16),
         vmem((NEAR * CL, CS), F32),
-        vmem((CL, RANK * RANK), F32),
         vmem((3, 2 * CL, 128), BF16),
         vmem((3, WINDOW, 2 * CL, 128), BF16),
         vmem((2, 128), F32),
@@ -501,11 +513,11 @@
         pltpu.SemaphoreType.DMA((5,)),
         pltpu.SemaphoreType.DMA((5,)),
     ]
-    pressure, gap = pl.pallas_call(
+    pressure, gap, direction, image, step = pl.pallas_call(
         kernel,
-        out_shape=[jax.ShapeDtypeStruct(fold_shape, F32)] * 2,
+        out_shape=[jax.ShapeDtypeStruct(fold_shape, F32)] * 5,
         in_specs=[pl.BlockSpec(memory_space=pl.ANY)] * 10,
-        out_specs=[pl.BlockSpec(memory_space=pltpu.VMEM)] * 2,
+        out_specs=[pl.BlockSpec(memory_space=pltpu.VMEM)] * 5,
         scratch_shapes=scratch,
         compiler_params=pltpu.CompilerParams(
             collective_id=0, has_side_effects=True, vmem_limit_bytes=60 * 2**20
@@ -520,8 +532,10 @@
         far_list,
         source_basis.reshape(CL * RANK, CS),
         target_basis.reshape(CL * RANK, CS),
-        coupling,
-    )
+        jnp.transpose(coupling, (1, 0, 2)),
+    )
+    pressure = pressure - step * direction
+    gap = gap - step * image
     return pressure.reshape(elements), gap.reshape(elements)
 
 

time: 55.6 us -> 49.1 us (0.88)
  local copies, waits for them, and re-layouts: 4.64 us -> 0 us
  Pallas kernels: 50.1 us -> 46.9 us
  other arithmetic: 0 us -> 1.37 us
    unnamed x3 -> x0, local copies, waits for them, and re-layouts: 4.64 us -> none
    pallas_call x1, Pallas kernels: 50.1 us -> 46.9 us  [shards(): pl.pallas_call(kernel, out_shape=[jax.ShapeDtypeStruct(fold_shape, F32)]...]
    reshape x0 -> x1, other arithmetic: none -> 1.37 us  [shards(): return (pressure.reshape(elements), gap.reshape(elements))]
where the time goes in v3:
time: 49.1 us; the launch traced here: 48.9 us
  Pallas kernels  46.9 us (96%)
  other arithmetic  1.37 us (3%)
  between operations  0.64 us (1%)
    pallas_call x1, Pallas kernels, shards(): pl.pallas_call(kernel, out_shape=[jax.ShapeDtypeStruct(fold_shape, F32)]...  46.9 us
    reshape x1, other arithmetic, shards(): return (pressure.reshape(elements), gap.reshape(elements))  1.37 us

profile of v3, /device:TPU:1, one launch (start us, length us, event | category | flops | bytes accessed | tf_op | source)
XLA Modules:
  0.0 48.9 jit_solution(3495272712890856169)
XLA Ops:
  0.6 46.9 %shard_map.113 = (f32[16,128]{1,0:T(8,128)}, f32[16,128]{1,0:T(8,128)}, f32[16,128]{1,0:T(8,128)}, f32[16,128]{1,0:T(8,128)}, f32[16,128]{1,0:T(8,128)}) custom-call(f32[16,128]{1,0:T(8,128)} %bitcast.14, f32[16,128]{1,0:T(8,128)} %bitcast.15, s32[16,128]{1,0:T(8,128)} %bitcast.16, f32[16,128]{1,0:T(8,128)} %bitcast.17, bf16[8,9,256,256]{3,2,1,0:T(8,128)(2,1)} %near_hbm.1, ...), custom_call_target="tpu_custom_call" | custom-call | tf_op jit(solution)/shard_map/pallas_call | solution.py:516
  47.5 1.4 %subtract_bitcast_fusion = (f32[2048]{0:T(1024)}, f32[2048]{0:T(1024)}) fusion(f32[16,128]{1,0:T(8,128)} %get-tuple-element.10, f32[16,128]{1,0:T(8,128)} %get-tuple-element.8, f32[16,128]{1,0:T(8,128)} %get-tuple-element.11, f32[16,128]{1,0:T(8,128)} %get-tuple-element.7, f32[16,128]{1,0:T(8,128)} %get-tuple-element.9), kind=kLoop, calls=%fused_computation | loop fusion | flops 8192 | bytes 57344 | tf_op jit(solution)/shard_map/reshape | solution.py:539

commit v4 on v3

--- a/solution.py
+++ b/solution.py
@@ -28,7 +28,7 @@
 
 
 FAR_FIRST = sorted(range(1, DEVICES), key=lambda slot: -hops(slot))
-FIELD_FIRST = sorted(range(1, WINDOW), key=lambda slot: -hops(slot % MEMBERS))
+FIELD_FIRST = sorted(range(MEMBERS), key=lambda slot: -hops(slot))
 
 
 def dot(a, b, dims=((1,), (0,))):
@@ -102,7 +102,6 @@
 
     groups = [lax.bitwise_and(g + 2 * dx, 6) + lax.bitwise_xor(lax.bitwise_and(g, 1), dc) for dx in range(4) for dc in range(2)]
     members = [around(dy, dz) for dy in range(4) for dz in range(4)]
-    sides = (g, lax.bitwise_and(g + 1, 7), lax.bitwise_and(g + 7, 7))
 
     def peer(slot):
         return groups[slot // MEMBERS], members[slot % MEMBERS]
@@ -146,6 +145,11 @@
         second = jnp.sum(jnp.where(own, product[CL:], 0.0), axis=0, keepdims=True)
         return first, second
 
+    def project_fine(value):
+        high = value.astype(BF16).astype(F32)
+        first, second = project(jnp.concatenate([high, value - high], axis=0).astype(BF16))
+        return first + second
+
     lane1 = lax.broadcasted_iota(jnp.int32, (1, 128), 1)
 
     def scalar_row(*values):
@@ -154,31 +158,39 @@
             row = jnp.where(lane1 == i, value, row)
         return row
 
-    def field_copy(phase, slot):
+    odd = lax.bitwise_and(g, 1)
+    partner = lax.bitwise_xor(g, 1)
+    across = lax.bitwise_and(g - 1 + 2 * odd, 7)
+
+    def field_copy(phase, kind, src, start, to, count=1):
         return pltpu.make_async_remote_copy(
-            src_ref=field_out.at[phase],
-            dst_ref=field_in.at[phase, slot],
-            send_sem=field_send.at[phase],
-            recv_sem=field_recv.at[phase],
-            device_id=(sides[slot // MEMBERS], members[slot % MEMBERS]),
+            src_ref=src,
+            dst_ref=field_in.at[phase, pl.ds(start, count)],
+            send_sem=field_send.at[phase, kind],
+            recv_sem=field_recv.at[phase, kind],
+            device_id=to,
             device_id_type=MESH,
         )
 
-    def field_all(phase):
-        rest = field_in.at[phase, pl.ds(1, WINDOW - 1)]
-        return pltpu.make_async_remote_copy(
-            src_ref=rest,
-            dst_ref=rest,
-            send_sem=field_send.at[phase],
-            recv_sem=field_recv.at[phase],
-            device_id=peer(1),
-            device_id_type=MESH,
-        )
+    def field_all(phase, kind):
+        start, count = ((1, MEMBERS - 1), (MEMBERS, MEMBERS), (2 * MEMBERS, MEMBERS))[kind]
+        rest = field_in.at[phase, pl.ds(start, count)]
+        return field_copy(phase, kind, rest, start, peer(1), count)
+
+    def forward(phase):
+        field_all(phase, 0).wait_recv()
+        whole = field_in.at[phase, pl.ds(0, MEMBERS)]
+        field_copy(phase, 2, whole, (1 + odd) * MEMBERS, (partner, m), MEMBERS).start()
+
+    def field_here(phase):
+        forward(phase)
+        field_all(phase, 1).wait_recv()
+        field_all(phase, 2).wait_recv()
 
     def proj_copy(out, into, sem, slot):
         return pltpu.make_async_remote_copy(
             src_ref=out,
-            dst_ref=into.at[slot],
+            dst_ref=into.at[pl.ds(slot * out.shape[0], out.shape[0])],
             send_sem=proj_send.at[sem],
             recv_sem=proj_recv.at[sem],
             device_id=peer(slot),
@@ -186,7 +198,8 @@
         )
 
     def proj_all(into, sem):
-        rest = into.at[pl.ds(1, DEVICES - 1)]
+        each = into.shape[0] // DEVICES
+        rest = into.at[pl.ds(each, (DEVICES - 1) * each)]
         return pltpu.make_async_remote_copy(
             src_ref=rest,
             dst_ref=rest,
@@ -198,15 +211,19 @@
 
     def send_field(phase, value):
         block = tall(value).astype(BF16)
-        field_out[phase] = block
+        field_out[phase, 0] = block
         field_in[phase, 0] = block
+        src = field_out.at[phase]
         for slot in FIELD_FIRST:
-            field_copy(phase, slot).start()
+            if slot:
+                field_copy(phase, 0, src, slot, (g, members[slot])).start()
+        for slot in FIELD_FIRST:
+            field_copy(phase, 1, src, (2 - odd) * MEMBERS + slot, (across, members[slot])).start()
 
     def send_proj(out, into, sem, rows):
         for i, row in enumerate(rows):
             out[i : i + 1, :] = row
-            into[0, i : i + 1, :] = row
+            into[i : i + 1, :] = row
         for slot in FAR_FIRST:
             proj_copy(out, into, sem, slot).start()
 
@@ -315,22 +332,26 @@
         summed = jnp.zeros((CL, RANK * RANK), F32)
         for f in range(FAR):
             summed = summed + spreaded[f * CL : (f + 1) * CL] * coupling_v[f].astype(F32)
-        hi, mid, low = split3(summed)
-        coupled = dot(hi, fold[...]) + (dot(mid, fold[...]) + dot(low, fold[...]))
+        high = summed.astype(BF16).astype(F32)
+        both = dot(jnp.concatenate([high, summed - high], axis=0).astype(BF16), fold[...])
+        coupled = both[:CL] + both[CL:]
         return dot(jnp.where(own, coupled, 0.0).astype(BF16), target_v[...])
 
     def operate(value, products, projected):
         narrow = value.astype(BF16).astype(F32)
         return compliance * narrow + (slot_sum(products) + far_sum(projected))
 
+    def rows_of(ref, i):
+        return ref[pl.ds(i, DEVICES, stride=ref.shape[0] // DEVICES), :]
+
     def proj_rows(ref):
-        return jnp.concatenate([ref[:, 0, :], ref[:, 1, :]], axis=1)
+        return jnp.concatenate([rows_of(ref, 0), rows_of(ref, 1)], axis=1)
 
     def near_scalars(scalars):
-        hi, mid, low = split3(scalars)
-        return dot(near_dev[...], hi) + (dot(near_dev[...], mid) + dot(near_dev[...], low))
-
-    field_all(0).wait_recv()
+        picked = dot(near_dev[...], jnp.concatenate(split3(scalars), axis=1))
+        return picked[:, :128] + (picked[:, 128:256] + picked[:, 256:])
+
+    field_here(0)
     rows0 = gather_field(0)
     mask_rows = jnp.where(rows0 != 0.0, 1.0, 0.0)
     near0 = near_products(rows0)
@@ -342,8 +363,7 @@
     gap_centre = gap_sum / safe_count
     local = (gap - gap_centre) * mask
     send_field(1, local)
-    zeros = jnp.zeros_like(local)
-    first, _ = project(jnp.concatenate([local, zeros], axis=0).astype(BF16))
+    first = project_fine(local)
     send_proj(
         proj_out.at[1],
         proj_in.at[1],
@@ -354,13 +374,13 @@
     mask_near = near_products(mask_rows)
     proj_all(proj_in.at[0], 1).wait_recv()
     mask_projs = proj_rows(proj_in.at[0])
-    counts = proj_in[0, :, 2, :][:, 0:1]
+    counts = rows_of(proj_in.at[0], 2)[:, 0:1]
     count = jnp.sum(counts, axis=0, keepdims=True)
 
-    field_all(1).wait_recv()
+    field_here(1)
     near1 = near_products(gather_field(1))
     proj_all(proj_in.at[1], 2).wait_recv()
-    scalars = proj_in[1, :, 2, :]
+    scalars = rows_of(proj_in.at[1], 2)
     gap_mean = jnp.sum(scalars[:, 0:1], axis=0, keepdims=True) / count
     direction = (gap - gap_mean) * mask
     here = near_scalars(scalars)
@@ -372,10 +392,12 @@
     image_centre = image_sum / safe_count
     centred = (image - image_centre) * mask
     norm_own = total(direction * direction)
-    fit = total(centred * direction) / jnp.where(norm_own > 0.0, norm_own, 1.0)
+    direction_sum = total(mask * direction)
+    cross = total(mask * image * direction)
+    fit = (cross - image_centre * direction_sum) / jnp.where(norm_own > 0.0, norm_own, 1.0)
     local = centred - fit * direction
     send_field(2, local)
-    first, _ = project(jnp.concatenate([local, zeros], axis=0).astype(BF16))
+    first = project_fine(local)
     small = centred * SCALE
     send_proj(
         proj_out.at[2],
@@ -386,8 +408,8 @@
             first[:, 128:],
             scalar_row(
                 image_sum,
-                total(mask * image * direction),
-                total(mask * direction),
+                cross,
+                direction_sum,
                 norm_own,
                 total(small * small),
                 image_centre,
@@ -396,10 +418,10 @@
         ),
     )
 
-    field_all(2).wait_recv()
+    field_here(2)
     near2 = near_products(gather_field(2))
     proj_all(proj_in.at[2], 3).wait_recv()
-    scalars = proj_in[2, :, 2, :]
+    scalars = rows_of(proj_in.at[2], 2)
     sums = jnp.sum(scalars, axis=0, keepdims=True)
     image_mean = sums[:, 0:1] / count
     norm_old = sums[:, 3:4]
@@ -453,13 +475,14 @@
         ),
     )
     proj_all(last_in, 4).wait_recv()
-    sums = jnp.sum(last_in[:, 0, :], axis=0, keepdims=True)
+    sums = jnp.sum(last_in[...], axis=0, keepdims=True)
     image_mean = sums[:, 0:1] / count
     step = sums[:, 3:4] / (sums[:, 1:2] - image_mean * sums[:, 2:3])
     step_out[...] = jnp.broadcast_to(step, step_out.shape)
 
     for phase in range(3):
-        field_all(phase).wait_send()
+        for kind in range(3):
+            field_all(phase, kind).wait_send()
     proj_all(proj0_in, 0).wait_send()
     for i in range(3):
         proj_all(proj_in.at[i], i + 1).wait_send()
@@ -499,17 +522,17 @@
         vmem((CS, RANK * RANK), BF16),
         vmem((RANK * RANK, CS), BF16),
         vmem((NEAR * CL, CS), F32),
-        vmem((3, 2 * CL, 128), BF16),
+        vmem((3, 1, 2 * CL, 128), BF16),
         vmem((3, WINDOW, 2 * CL, 128), BF16),
         vmem((2, 128), F32),
-        vmem((DEVICES, 2, 128), F32),
+        vmem((DEVICES * 2, 128), F32),
         vmem((3, 3, 128), F32),
-        vmem((3, DEVICES, 3, 128), F32),
+        vmem((3, DEVICES * 3, 128), F32),
         vmem((1, 128), F32),
-        vmem((DEVICES, 1, 128), F32),
+        vmem((DEVICES, 128), F32),
         pltpu.SemaphoreType.DMA((10,)),
-        pltpu.SemaphoreType.DMA((3,)),
-        pltpu.SemaphoreType.DMA((3,)),
+        pltpu.SemaphoreType.DMA((3, 3)),
+        pltpu.SemaphoreType.DMA((3, 3)),
         pltpu.SemaphoreType.DMA((5,)),
         pltpu.SemaphoreType.DMA((5,)),
     ]

time: 49.1 us -> 47.4 us (0.965)
  Pallas kernels: 46.9 us -> 45.2 us
    pallas_call x1, Pallas kernels: 46.9 us -> 45.2 us  [shards(): pl.pallas_call(kernel, out_shape=[jax.ShapeDtypeStruct(fold_shape, F32)]...]
where the time goes in v4:
time: 47.4 us; the launch traced here: 47.2 us
  Pallas kernels  45.2 us (95%)
  other arithmetic  1.37 us (3%)
  between operations  0.64 us (1%)
    pallas_call x1, Pallas kernels, shards(): pl.pallas_call(kernel, out_shape=[jax.ShapeDtypeStruct(fold_shape, F32)]...  45.2 us
    reshape x1, other arithmetic, shards(): return (pressure.reshape(elements), gap.reshape(elements))  1.37 us

profile of v4, /device:TPU:1, one launch (start us, length us, event | category | flops | bytes accessed | tf_op | source)
XLA Modules:
  0.0 47.2 jit_solution(3280206634260335887)
XLA Ops:
  0.6 45.2 %shard_map.113 = (f32[16,128]{1,0:T(8,128)}, f32[16,128]{1,0:T(8,128)}, f32[16,128]{1,0:T(8,128)}, f32[16,128]{1,0:T(8,128)}, f32[16,128]{1,0:T(8,128)}) custom-call(f32[16,128]{1,0:T(8,128)} %bitcast.14, f32[16,128]{1,0:T(8,128)} %bitcast.15, s32[16,128]{1,0:T(8,128)} %bitcast.16, f32[16,128]{1,0:T(8,128)} %bitcast.17, bf16[8,9,256,256]{3,2,1,0:T(8,128)(2,1)} %near_hbm.1, ...), custom_call_target="tpu_custom_call" | custom-call | tf_op jit(solution)/shard_map/pallas_call | solution.py:539
  45.8 1.4 %subtract_bitcast_fusion = (f32[2048]{0:T(1024)}, f32[2048]{0:T(1024)}) fusion(f32[16,128]{1,0:T(8,128)} %get-tuple-element.10, f32[16,128]{1,0:T(8,128)} %get-tuple-element.8, f32[16,128]{1,0:T(8,128)} %get-tuple-element.11, f32[16,128]{1,0:T(8,128)} %get-tuple-element.7, f32[16,128]{1,0:T(8,128)} %get-tuple-element.9), kind=kLoop, calls=%fused_computation | loop fusion | flops 8192 | bytes 57344 | tf_op jit(solution)/shard_map/reshape | solution.py:562

commit v5 on v4

--- a/solution.py
+++ b/solution.py
@@ -281,12 +281,6 @@
     pl.semaphore_wait(barrier, DEVICES - 1)
     send_field(0, pressure)
     send_proj(proj0_out, proj0_in, 0, (first[:, :128], first[:, 128:]))
-    send_proj(
-        proj_out.at[0],
-        proj_in.at[0],
-        1,
-        (mask_proj[:, :128], mask_proj[:, 128:], scalar_row(count_own)),
-    )
 
     for load in loads[5:]:
         load.wait()
@@ -354,6 +348,12 @@
     field_here(0)
     rows0 = gather_field(0)
     mask_rows = jnp.where(rows0 != 0.0, 1.0, 0.0)
+    send_proj(
+        proj_out.at[0],
+        proj_in.at[0],
+        1,
+        (mask_proj[:, :128], mask_proj[:, 128:], scalar_row(count_own)),
+    )
     near0 = near_products(rows0)
     proj_all(proj0_in, 0).wait_recv()
     gap = operate(pressure, near0, proj_rows(proj0_in)) - height

time: 47.4 us -> 47.1 us (level)
  no operation moved by 1% of the time
where the time goes in v5:
time: 47.1 us; the launch traced here: 46.9 us
  Pallas kernels  44.9 us (95%)
  other arithmetic  1.37 us (3%)
  between operations  0.64 us (1%)
    pallas_call x1, Pallas kernels, shards(): pl.pallas_call(kernel, out_shape=[jax.ShapeDtypeStruct(fold_shape, F32)]...  44.9 us
    reshape x1, other arithmetic, shards(): return (pressure.reshape(elements), gap.reshape(elements))  1.37 us

profile of v5, /device:TPU:1, one launch (start us, length us, event | category | flops | bytes accessed | tf_op | source)
XLA Modules:
  0.0 46.9 jit_solution(7981348589772217976)
XLA Ops:
  0.6 44.9 %shard_map.113 = (f32[16,128]{1,0:T(8,128)}, f32[16,128]{1,0:T(8,128)}, f32[16,128]{1,0:T(8,128)}, f32[16,128]{1,0:T(8,128)}, f32[16,128]{1,0:T(8,128)}) custom-call(f32[16,128]{1,0:T(8,128)} %bitcast.14, f32[16,128]{1,0:T(8,128)} %bitcast.15, s32[16,128]{1,0:T(8,128)} %bitcast.16, f32[16,128]{1,0:T(8,128)} %bitcast.17, bf16[8,9,256,256]{3,2,1,0:T(8,128)(2,1)} %near_hbm.1, ...), custom_call_target="tpu_custom_call" | custom-call | tf_op jit(solution)/shard_map/pallas_call | solution.py:539
  45.5 1.4 %subtract_bitcast_fusion = (f32[2048]{0:T(1024)}, f32[2048]{0:T(1024)}) fusion(f32[16,128]{1,0:T(8,128)} %get-tuple-element.10, f32[16,128]{1,0:T(8,128)} %get-tuple-element.8, f32[16,128]{1,0:T(8,128)} %get-tuple-element.11, f32[16,128]{1,0:T(8,128)} %get-tuple-element.7, f32[16,128]{1,0:T(8,128)} %get-tuple-element.9), kind=kLoop, calls=%fused_computation | loop fusion | flops 8192 | bytes 57344 | tf_op jit(solution)/shard_map/reshape | solution.py:562

commit v6 on v5

--- a/solution.py
+++ b/solution.py
@@ -146,9 +146,9 @@
         return first, second
 
     def project_fine(value):
-        high = value.astype(BF16).astype(F32)
-        first, second = project(jnp.concatenate([high, value - high], axis=0).astype(BF16))
-        return first + second
+        product = dot(jnp.concatenate(split3(value), axis=0), source_v[...], ((1,), (1,)))
+        product = product[:CL] + (product[CL : 2 * CL] + product[2 * CL :])
+        return jnp.sum(jnp.where(own, product, 0.0), axis=0, keepdims=True)
 
     lane1 = lax.broadcasted_iota(jnp.int32, (1, 128), 1)
 
@@ -359,11 +359,11 @@
     gap = operate(pressure, near0, proj_rows(proj0_in)) - height
 
     safe_count = jnp.maximum(count_own, 1.0)
+    first = project_fine(mask * gap)
     gap_sum = total(mask * gap)
     gap_centre = gap_sum / safe_count
     local = (gap - gap_centre) * mask
     send_field(1, local)
-    first = project_fine(local)
     send_proj(
         proj_out.at[1],
         proj_in.at[1],
@@ -385,9 +385,10 @@
     direction = (gap - gap_mean) * mask
     here = near_scalars(scalars)
     near1 = near1 + (here[:, 1:2] - gap_mean) * mask_near
-    projs1 = proj_rows(proj_in.at[1]) + (scalars[:, 1:2] - gap_mean) * mask_projs
+    projs1 = proj_rows(proj_in.at[1]) - gap_mean * mask_projs
     image = operate(direction, near1, projs1)
 
+    first = project_fine(mask * image)
     image_sum = total(mask * image)
     image_centre = image_sum / safe_count
     centred = (image - image_centre) * mask
@@ -397,7 +398,6 @@
     fit = (cross - image_centre * direction_sum) / jnp.where(norm_own > 0.0, norm_own, 1.0)
     local = centred - fit * direction
     send_field(2, local)
-    first = project_fine(local)
     small = centred * SCALE
     send_proj(
         proj_out.at[2],
@@ -445,10 +445,8 @@
         - step * near2
         - step * (here[:, 5:6] - image_mean) * mask_near
     )
-    projs2 = (
-        (1.0 + ratio - step * scalars[:, 6:7]) * projs1
-        - step * proj_rows(proj_in.at[2])
-        - step * shifts * mask_projs
+    projs2 = (1.0 + ratio) * projs1 - step * (
+        proj_rows(proj_in.at[2]) - image_mean * mask_projs
     )
     image = operate(direction, near2, projs2)
 

time: 47.1 us -> 46.7 us (level)
  no operation moved by 1% of the time
where the time goes in v6:
time: 46.7 us; the launch traced here: 46.5 us
  Pallas kernels  44.5 us (95%)
  other arithmetic  1.37 us (3%)
  between operations  0.64 us (1%)
    pallas_call x1, Pallas kernels, shards(): pl.pallas_call(kernel, out_shape=[jax.ShapeDtypeStruct(fold_shape, F32)]...  44.5 us
    reshape x1, other arithmetic, shards(): return (pressure.reshape(elements), gap.reshape(elements))  1.37 us

profile of v6, /device:TPU:1, one launch (start us, length us, event | category | flops | bytes accessed | tf_op | source)
XLA Modules:
  0.0 46.5 jit_solution(5472880592591675159)
XLA Ops:
  0.6 44.5 %shard_map.113 = (f32[16,128]{1,0:T(8,128)}, f32[16,128]{1,0:T(8,128)}, f32[16,128]{1,0:T(8,128)}, f32[16,128]{1,0:T(8,128)}, f32[16,128]{1,0:T(8,128)}) custom-call(f32[16,128]{1,0:T(8,128)} %bitcast.14, f32[16,128]{1,0:T(8,128)} %bitcast.15, s32[16,128]{1,0:T(8,128)} %bitcast.16, f32[16,128]{1,0:T(8,128)} %bitcast.17, bf16[8,9,256,256]{3,2,1,0:T(8,128)(2,1)} %near_hbm.1, ...), custom_call_target="tpu_custom_call" | custom-call | tf_op jit(solution)/shard_map/pallas_call | solution.py:537
  45.2 1.4 %subtract_bitcast_fusion = (f32[2048]{0:T(1024)}, f32[2048]{0:T(1024)}) fusion(f32[16,128]{1,0:T(8,128)} %get-tuple-element.10, f32[16,128]{1,0:T(8,128)} %get-tuple-element.8, f32[16,128]{1,0:T(8,128)} %get-tuple-element.11, f32[16,128]{1,0:T(8,128)} %get-tuple-element.7, f32[16,128]{1,0:T(8,128)} %get-tuple-element.9), kind=kLoop, calls=%fused_computation | loop fusion | flops 8192 | bytes 57344 | tf_op jit(solution)/shard_map/reshape | solution.py:560

commit v7 on v6

--- a/solution.py
+++ b/solution.py
@@ -271,7 +271,7 @@
         picks.append(jnp.where(dev_iota == far_row[:, f : f + 1], 1.0, 0.0))
         parts.append(jnp.where(part_iota == far_part[:, f : f + 1], 1.0, 0.0))
     far_pick[...] = jnp.concatenate(picks, axis=0).astype(BF16)
-    far_seg[...] = jnp.concatenate(parts, axis=0)
+    far_seg[...] = jnp.concatenate(parts, axis=0).astype(BF16)
     tall_iota = lax.bitwise_and(lax.broadcasted_iota(jnp.int32, (CS, RANK * RANK), 0), RANK - 1)
     wide_iota = lax.bitwise_and(lax.broadcasted_iota(jnp.int32, (CS, RANK * RANK), 1), RANK - 1)
     spread[...] = jnp.where(tall_iota == wide_iota, 1.0, 0.0).astype(BF16)
@@ -294,7 +294,7 @@
 
     lax.fori_loop(0, CL, turn, 0)
 
-    row16 = lax.broadcasted_iota(jnp.int32, (2 * CL, CS), 0)
+    row16 = row8
 
     def gather_field(phase):
         window = field_in[phase].reshape(WINDOW * 2 * CL, 128)
@@ -306,7 +306,7 @@
         rows_v[...] = rows
         products = []
         for n in range(NEAR):
-            acc = jnp.zeros((2 * CL, CS), F32)
+            acc = jnp.zeros((CL, CS), F32)
             for c in range(CL):
                 row = rows_v[n * CL + c : n * CL + c + 1, :]
                 left = jnp.where(row16 == c, row, 0.0).astype(BF16)
@@ -322,7 +322,7 @@
 
     def far_sum(projected):
         picked = dot(far_pick[...], projected.astype(BF16))
-        spreaded = dot((picked * far_seg[...]).astype(BF16), spread[...])
+        spreaded = dot(picked.astype(BF16) * far_seg[...], spread[...])
         summed = jnp.zeros((CL, RANK * RANK), F32)
         for f in range(FAR):
             summed = summed + spreaded[f * CL : (f + 1) * CL] * coupling_v[f].astype(F32)
@@ -516,7 +516,7 @@
         vmem((2 * NEAR * CL, WINDOW * 2 * CL), BF16),
         vmem((NEAR * CL, DEVICES), BF16),
         vmem((FAR * CL, DEVICES), BF16),
-        vmem((FAR * CL, CS), F32),
+        vmem((FAR * CL, CS), BF16),
         vmem((CS, RANK * RANK), BF16),
         vmem((RANK * RANK, CS), BF16),
         vmem((NEAR * CL, CS), F32),

time: 46.7 us -> 46.7 us (level)
  no operation moved by 1% of the time
where the time goes in v7:
time: 46.7 us; the launch traced here: 46.5 us
  Pallas kernels  44.5 us (95%)
  other arithmetic  1.37 us (3%)
  between operations  0.64 us (1%)
    pallas_call x1, Pallas kernels, shards(): pl.pallas_call(kernel, out_shape=[jax.ShapeDtypeStruct(fold_shape, F32)]...  44.5 us
    reshape x1, other arithmetic, shards(): return (pressure.reshape(elements), gap.reshape(elements))  1.37 us

profile of v7, /device:TPU:1, one launch (start us, length us, event | category | flops | bytes accessed | tf_op | source)
XLA Modules:
  0.0 46.5 jit_solution(18314485406811310627)
XLA Ops:
  0.6 44.5 %shard_map.113 = (f32[16,128]{1,0:T(8,128)}, f32[16,128]{1,0:T(8,128)}, f32[16,128]{1,0:T(8,128)}, f32[16,128]{1,0:T(8,128)}, f32[16,128]{1,0:T(8,128)}) custom-call(f32[16,128]{1,0:T(8,128)} %bitcast.14, f32[16,128]{1,0:T(8,128)} %bitcast.15, s32[16,128]{1,0:T(8,128)} %bitcast.16, f32[16,128]{1,0:T(8,128)} %bitcast.17, bf16[8,9,256,256]{3,2,1,0:T(8,128)(2,1)} %near_hbm.1, ...), custom_call_target="tpu_custom_call" | custom-call | tf_op jit(solution)/shard_map/pallas_call | solution.py:537
  45.2 1.4 %subtract_bitcast_fusion = (f32[2048]{0:T(1024)}, f32[2048]{0:T(1024)}) fusion(f32[16,128]{1,0:T(8,128)} %get-tuple-element.10, f32[16,128]{1,0:T(8,128)} %get-tuple-element.8, f32[16,128]{1,0:T(8,128)} %get-tuple-element.11, f32[16,128]{1,0:T(8,128)} %get-tuple-element.7, f32[16,128]{1,0:T(8,128)} %get-tuple-element.9), kind=kLoop, calls=%fused_computation | loop fusion | flops 8192 | bytes 57344 | tf_op jit(solution)/shard_map/reshape | solution.py:560
